TPU v7x, 256 devices: a whole 4x4x8 slice. The times are simulated.
256 devices in a mesh: tm: 4 (over y), space: 64 (over z, x, core).
Axes of the slice: x: 4, y: 4, z: 8, core: 2. Of those that a mesh axis runs over, the one named last changes fastest.
Arguments:
- latents: bfloat16 [4, 64, 8, 40, 384], P('tm', 'space'), may hold values from -8 to 8
- gain_first: float32 [384], replicated, may hold values from 0.5 to 2
- shift_first: float32 [384], replicated, may hold values from -3 to 3
- kernel_first: bfloat16 [3, 3, 3, 384, 384], P(None, None, None, 'space', 'tm'), may hold values from -0.0625 to 0.0625
- bias_first: float32 [384], replicated, may hold values from -3 to 3
- gain_second: float32 [384], replicated, may hold values from 0.5 to 2
- shift_second: float32 [384], replicated, may hold values from -3 to 3
- kernel_second: bfloat16 [3, 3, 3, 384, 384], P(None, None, None, 'space', 'tm'), may hold values from -0.0625 to 0.0625
- bias_second: float32 [384], replicated, may hold values from -3 to 3
Outputs:
- decoded: bfloat16 [4, 64, 8, 40, 384], P('tm', 'space')
All inputs are finite; a program needn't handle non-finite values.
Results may differ from a plain program's by a relative error of at most 0.0085.
Values may be sent and summed in bfloat16 or wider, within the bound.
No kernel may reach another device: no remote copies, remote signals or barrier semaphores. Data moves between devices by JAX's collectives and lax.ppermute only.
A program may use at most 128 MiB of HBM per device.

v0:
```python
import jax
import jax.numpy as jnp
from jax import lax
from jax.sharding import PartitionSpec as P

GROUPS = 32
GX = 8
EPS = 1e-06


def shifted(value, axis, steps):
    count = lax.axis_size(axis)
    initial, last = (max(0, -steps), min(count, count - steps))
    return lax.ppermute(value, axis, [(source, source + steps) for source in range(initial, last)])


def spatial_halo(tile):
    column = lax.axis_index("space") % GX
    from_west = shifted(tile[:, -1:, :], "space", 1)
    from_east = shifted(tile[:, :1, :], "space", -1)
    from_west = jnp.where(column > 0, from_west, jnp.zeros_like(from_west))
    from_east = jnp.where(column < GX - 1, from_east, jnp.zeros_like(from_east))
    widened = jnp.concatenate([from_west, tile, from_east], axis=1)
    from_north = shifted(widened[-1:], "space", GX)
    from_south = shifted(widened[:1], "space", -GX)
    return jnp.concatenate([from_north, widened, from_south], axis=0)


def group_act(field, gain, shift, count):
    width = field.shape[-1] // GROUPS
    grouped = field.reshape(-1, GROUPS, width)
    total = lax.psum(jnp.sum(grouped, axis=(0, 2)), ("tm", "space"))
    mean = total / count
    centered = grouped - mean[None, :, None]
    squares = lax.psum(jnp.sum(centered * centered, axis=(0, 2)), ("tm", "space"))
    spread = squares / count
    normed = (centered * lax.rsqrt(spread + EPS)[None, :, None]).reshape(field.shape)
    return jax.nn.silu(normed * gain + shift).astype(jnp.bfloat16)


def apply_taps(stack, kernel, frames_out, rows, cols):
    width = kernel.shape[3]
    total = None
    for step_t in range(3):
        for step_y in range(3):
            for step_x in range(3):
                window = stack[
                    step_t : step_t + frames_out, step_y : step_y + rows, step_x : step_x + cols, :
                ]
                term = jnp.dot(
                    window.reshape(-1, width),
                    kernel[step_t, step_y, step_x],
                    preferred_element_type=jnp.float32,
                )
                total = term if total is None else total + term
    return total


def relay_frame(padded):
    return shifted(padded, "tm", 1)


def conv_near(act, kernel_cols, bias):
    rows, cols, channels = act.shape
    padded = spatial_halo(act)
    previous = relay_frame(padded)
    earlier = relay_frame(previous)
    stack = jnp.stack([earlier, previous, padded])
    kernel_full = lax.all_gather(kernel_cols, "space", axis=3, tiled=True)
    total = apply_taps(stack, kernel_full, 1, rows, cols)
    return total.reshape(rows, cols, channels) + bias


def shards(
    latents,
    gain_first,
    shift_first,
    kernel_first,
    bias_first,
    gain_second,
    shift_second,
    kernel_second,
    bias_second,
):
    tile = latents[0, 0].astype(jnp.float32)
    rows, cols, channels = tile.shape
    count = float(lax.axis_size("tm") * lax.axis_size("space") * rows * cols * (channels // GROUPS))
    first_act = group_act(tile, gain_first, shift_first, count)
    cols_first, cols_second = (
        lax.all_gather(kernel_first, "tm", axis=4, tiled=True),
        lax.all_gather(kernel_second, "tm", axis=4, tiled=True),
    )
    first_out = conv_near(first_act, cols_first, bias_first)
    second_act = group_act(first_out, gain_second, shift_second, count)
    second_out = conv_near(second_act, cols_second, bias_second)
    return (tile + second_out).astype(jnp.bfloat16)[None, None]


def solution(mesh):
    placed = (
        P("tm", "space", None, None, None),
        P(),
        P(),
        P(None, None, None, "space", "tm"),
        P(),
        P(),
        P(),
        P(None, None, None, "space", "tm"),
        P(),
    )
    return jax.shard_map(
        shards,
        mesh=mesh,
        in_specs=placed,
        out_specs=P("tm", "space", None, None, None),
        check_vma=False,
    )
```

profile of v0, /device:TPU:62, one launch (start us, length us, event | category | flops | bytes accessed | tf_op | source)
XLA Modules:
  0.0 541.0 jit_solution(8671705609608427689)
XLA Ops:
  6.5 2.2 copy.14
  8.8 32.9 %all_gather.12 = bf16[3,3,3,6,384]{3,2,1,0,4:T(4,128)(2,1)S(1)} all-gather(bf16[3,3,3,6,96]{3,2,1,0,4:T(4,128)(2,1)} %copy.14), channel_id=1, replica_groups=mesh['tm'=4,'space'=64] {'tm'}, dimensions={4}, use_global_device_ids=true | all-gather | bytes 155520 | tf_op jit(solution)/shard_map/all_gather | solution.py:90
  41.7 4.8 copy.15
  46.5 2.2 copy.43
  48.8 32.0 %all_gather.14 = bf16[3,3,3,6,384]{3,2,1,0,4:T(4,128)(2,1)S(1)} all-gather(bf16[3,3,3,6,96]{3,2,1,0,4:T(4,128)(2,1)} %copy.43), channel_id=1, replica_groups=mesh['tm'=4,'space'=64] {'tm'}, dimensions={4}, use_global_device_ids=true | all-gather | bytes 155520 | tf_op jit(solution)/shard_map/all_gather | solution.py:91
  80.8 4.8 copy.44
  85.6 1.0 convert_reduce_fusion
  86.9 75.1 %psum.28 = f32[32]{0:T(128)S(1)} all-reduce(f32[32]{0:T(128)S(1)} %reduce_sum.51), channel_id=1, replica_groups=mesh['tm'=4,'space'=64] {'tm','space'}, use_global_device_ids=true, to_apply=%region_2.0 | all-reduce | flops 32 | bytes 256 | tf_op jit(solution)/shard_map/psum | solution.py:32
  162.2 1.0 fusion.35
  163.4 75.1 %psum.29 = f32[32]{0:T(128)S(1)} all-reduce(f32[32]{0:T(128)S(1)} %reduce_sum.54), channel_id=1, replica_groups=mesh['tm'=4,'space'=64] {'tm','space'}, use_global_device_ids=true, to_apply=%region_5.6 | all-reduce | flops 32 | bytes 256 | tf_op jit(solution)/shard_map/psum | solution.py:35
  238.8 1.1 fusion.46
  239.9 2.5 collective-permute-start
  242.4 3.1 collective-permute-start.1
  245.6 1.3 collective-permute-done.1
  246.9 3.7 collective-permute-start.2
  250.6 2.5 collective-permute-start.3
  253.2 3.3 collective-permute-done.3
  256.6 1.3 collective-permute-start.4
  258.0 8.4 %collective-permute-done.4 = bf16[10,42,384]{2,1,0:T(8,128)(2,1)S(1)} collective-permute-done((bf16[10,42,384]{2,1,0:T(8,128)(2,1)S(1)}, bf16[10,42,384]{2,1,0:T(8,128)(2,1)S(1)}, u32[]{:S(2)}, u32[]{:S(2)}) %collective-permute-start.4) | collective-permute-done | bytes 322592 | tf_op jit(solution)/shard_map/ppermute | solution.py:14
  266.4 1.3 collective-permute-start.5
  268.0 1.4 fusion.92
  269.5 7.9 %collective-permute-done.5 = bf16[10,42,384]{2,1,0:T(8,128)(2,1)S(1)} collective-permute-done((bf16[10,42,384]{2,1,0:T(8,128)(2,1)S(1)}, bf16[10,42,384]{2,1,0:T(8,128)(2,1)S(1)}, u32[]{:S(2)}, u32[]{:S(2)}) %collective-permute-start.5) | collective-permute-done | bytes 322592 | tf_op jit(solution)/shard_map/ppermute | solution.py:14
  277.4 1.1 fusion.91
  278.6 16.8 %fusion.85 = (bf16[1,1,1,384,384]{4,2,1,0,3:T(2,128)(2,1)S(1)}, bf16[1,1,1,384,384]{4,2,1,0,3:T(2,128)(2,1)S(1)}, bf16[1,1,1,384,384]{4,2,1,0,3:T(2,128)(2,1)S(1...) fusion(bf16[3,3,3,384,384]{4,2,1,0,3:T(4,128)(2,1)} %all-gather, ...), kind=kLoop, calls=%fused_computation.180 | loop fusion | bytes 11206656 | tf_op jit(solution)/shard_map/slice | solution.py:52
  299.2 7.0 %fusion.86 = (bf16[1,1,1,384,384]{4,2,1,0,3:T(2,128)(2,1)S(1)}, bf16[1,1,1,384,384]{4,2,1,0,3:T(2,128)(2,1)S(1)}, bf16[1,1,1,384,384]{4,2,1,0,3:T(2,128)(2,1)S(1...) fusion(bf16[3,3,3,384,384]{4,2,1,0,3:T(4,128)(2,1)} %all-gather, ...), kind=kLoop, calls=%fused_computation.181 | loop fusion | bytes 4718592 | tf_op jit(solution)/shard_map/slice | solution.py:52
  307.6 0.3 fusion.80
  308.6 0.8 fusion.27
  309.4 0.3 convolution_add_fusion.16
  311.8 0.4 add_reduce_fusion
  312.4 77.7 %psum.30 = f32[32]{0:T(128)S(1)} all-reduce(f32[32]{0:T(128)S(1)} %reduce_sum.72), channel_id=1, replica_groups=mesh['tm'=4,'space'=64] {'tm','space'}, use_global_device_ids=true, to_apply=%region_8.9 | all-reduce | flops 32 | bytes 256 | tf_op jit(solution)/shard_map/psum | solution.py:32
  390.5 72.8 %psum.31 = f32[32]{0:T(128)S(1)} all-reduce(f32[32]{0:T(128)S(1)} %reduce_sum.75), channel_id=1, replica_groups=mesh['tm'=4,'space'=64] {'tm','space'}, use_global_device_ids=true, to_apply=%region_11.12 | all-reduce | flops 32 | bytes 256 | tf_op jit(solution)/shard_map/psum | solution.py:35
  463.7 2.0 collective-permute-start.6
  465.7 3.6 collective-permute-start.7
  469.3 16.3 %fusion.83 = (bf16[1,1,1,384,384]{4,2,1,0,3:T(2,128)(2,1)S(1)}, bf16[1,1,1,384,384]{4,2,1,0,3:T(2,128)(2,1)S(1)}, bf16[1,1,1,384,384]{4,2,1,0,3:T(2,128)(2,1)S(1...) fusion(bf16[3,3,3,384,384]{4,2,1,0,3:T(4,128)(2,1)} %all-gather, ...), kind=kLoop, calls=%fused_computation.178 | loop fusion | bytes 11206656 | tf_op jit(solution)/shard_map/slice | solution.py:52
  485.8 1.9 collective-permute-start.8
  487.7 3.9 collective-permute-start.9
  491.6 6.9 %fusion.84 = (bf16[1,1,1,384,384]{4,2,1,0,3:T(2,128)(2,1)S(1)}, bf16[1,1,1,384,384]{4,2,1,0,3:T(2,128)(2,1)S(1)}, bf16[1,1,1,384,384]{4,2,1,0,3:T(2,128)(2,1)S(1...) fusion(bf16[3,3,3,384,384]{4,2,1,0,3:T(4,128)(2,1)} %all-gather, ...), kind=kLoop, calls=%fused_computation.179 | loop fusion | bytes 4718592 | tf_op jit(solution)/shard_map/slice | solution.py:52
  498.7 1.3 collective-permute-start.10
  500.7 11.3 %collective-permute-done.10 = bf16[10,42,384]{2,1,0:T(8,128)(2,1)S(1)} collective-permute-done((bf16[10,42,384]{2,1,0:T(8,128)(2,1)S(1)}, bf16[10,42,384]{2,1,0:T(8,128)(2,1)S(1)}, u32[]{:S(2)}, u32[]{:S(2)}) %collective-permute-start.10) | collective-permute-done | bytes 322592 | tf_op jit(solution)/shard_map/ppermute | solution.py:14
  512.9 0.3 fusion.54
  513.6 0.3 fusion.52
  514.3 0.3 fusion.50
  514.6 1.6 collective-permute-start.11
  516.5 0.3 fusion.48
  516.8 10.2 %collective-permute-done.11 = bf16[10,42,384]{2,1,0:T(8,128)(2,1)S(1)} collective-permute-done((bf16[10,42,384]{2,1,0:T(8,128)(2,1)S(1)}, bf16[10,42,384]{2,1,0:T(8,128)(2,1)S(1)}, u32[]{:S(2)}, u32[]{:S(2)}) %collective-permute-start.11) | collective-permute-done | bytes 322592 | tf_op jit(solution)/shard_map/ppermute | solution.py:14
  527.7 0.3 fusion.59
  530.1 0.7 fusion.33
  533.4 0.8 fusion.36
  (134 shorter events, 18.4 us)
Async XLA Ops:
  6.5 232.2 %copy-start.16 = (f32[384]{0:T(512)S(1)}, f32[384]{0:T(512)}, u32[]{:S(2)}) copy-start(f32[384]{0:T(512)} %param.10) | copy-start | bytes 4612
  6.5 232.2 %copy-start.15 = (f32[384]{0:T(512)S(1)}, f32[384]{0:T(512)}, u32[]{:S(2)}) copy-start(f32[384]{0:T(512)} %param.11) | copy-start | bytes 4612
  6.5 271.9 %all-gather.3.cloned.1.call-start = ((), (), s32[]{:S(2)}) async-start(), calls=%async_computation | async-start | bytes 10782720 | tf_op jit(solution)/shard_map/all_gather | solution.py:69
  46.5 422.8 %all-gather.5.cloned.1.call-start = ((), (), s32[]{:S(2)}) async-start(), calls=%async_computation.1 | async-start | bytes 10782720 | tf_op jit(solution)/shard_map/all_gather | solution.py:69
  239.9 5.6 %collective-permute-start = (bf16[8,1,384]{2,1,0:T(2,128)(2,1)S(1)}, bf16[8,1,384]{2,1,0:T(2,128)(2,1)S(1)}, u32[]{:S(2)}, u32[]{:S(2)}) collective-permute-start(bf16[8,1,384]{2,1,0:T(2,128)(2,1)S(1)} %get-tuple-element.119), channel_id=1, source_target_pairs={{0,1},{1,2},{2,3},{3,4},{4,5},{5,6},{6,7},{7,8},{8,9},{9,10},{10,1... | collective-permute-start | bytes 18440 | tf_op jit(solution)/shard_map/ppermute | solution.py:14
  242.4 4.5 collective-permute-start.1
  246.9 6.2 %collective-permute-start.2 = (bf16[1,42,384]{2,1,0:T(8,128)(2,1)S(1)}, bf16[1,42,384]{2,1,0:T(8,128)(2,1)S(1)}, u32[]{:S(2)}, u32[]{:S(2)}) collective-permute-start(bf16[1,42,384]{2,1,0:T(8,128)(2,1)S(1)} %get-tuple-element.115), channel_id=1, source_target_pairs={{0,8},{1,9},{2,10},{3,11},{4,12},{5,13},{6,14},{7,15},{8,16},{9,17... | collective-permute-start | bytes 96776 | tf_op jit(solution)/shard_map/ppermute | solution.py:14
  250.6 5.9 %collective-permute-start.3 = (bf16[1,42,384]{2,1,0:T(8,128)(2,1)S(1)}, bf16[1,42,384]{2,1,0:T(8,128)(2,1)S(1)}, u32[]{:S(2)}, u32[]{:S(2)}) collective-permute-start(bf16[1,42,384]{2,1,0:T(8,128)(2,1)S(1)} %get-tuple-element.116), channel_id=1, source_target_pairs={{8,0},{9,1},{10,2},{11,3},{12,4},{13,5},{14,6},{15,7},{16,8},{17,9... | collective-permute-start | bytes 96776 | tf_op jit(solution)/shard_map/ppermute | solution.py:14
  256.6 9.8 %collective-permute-start.4 = (bf16[10,42,384]{2,1,0:T(8,128)(2,1)S(1)}, bf16[10,42,384]{2,1,0:T(8,128)(2,1)S(1)}, u32[]{:S(2)}, u32[]{:S(2)}) collective-permute-start(bf16[10,42,384]{2,1,0:T(8,128)(2,1)S(1)} %pad_maximum_fusion), channel_id=1, source_target_pairs={{0,64},{64,128},{128,192},{1,65},{65,129},{129,193},{2,66},{66,130... | collective-permute-start | bytes 967688 | tf_op jit(solution)/shard_map/ppermute | solution.py:14
  266.4 10.9 %collective-permute-start.5 = (bf16[10,42,384]{2,1,0:T(8,128)(2,1)S(1)}, bf16[10,42,384]{2,1,0:T(8,128)(2,1)S(1)}, u32[]{:S(2)}, u32[]{:S(2)}) collective-permute-start(bf16[10,42,384]{2,1,0:T(8,128)(2,1)S(1)} %collective-permute-done.4), channel_id=1, source_target_pairs={{0,64},{64,128},{128,192},{1,65},{65,129},{129,193},{2,66},{66,130... | collective-permute-start | bytes 967688 | tf_op jit(solution)/shard_map/ppermute | solution.py:14
  278.5 16.9 %copy-start.13 = (bf16[1,8,40,384]{3,2,1,0:T(8,128)(2,1)S(1)}, bf16[1,8,40,384]{3,2,1,0:T(8,128)(2,1)}, u32[]{:S(2)}) copy-start(bf16[1,8,40,384]{3,2,1,0:T(8,128)(2,1)} %get-tuple-element.96) | copy-start | bytes 737284
  278.5 17.3 %copy-start.12 = (bf16[1,8,40,384]{3,2,1,0:T(8,128)(2,1)S(1)}, bf16[1,8,40,384]{3,2,1,0:T(8,128)(2,1)}, u32[]{:S(2)}) copy-start(bf16[1,8,40,384]{3,2,1,0:T(8,128)(2,1)} %get-tuple-element.105) | copy-start | bytes 737284
  278.5 17.6 %copy-start.11 = (bf16[1,8,40,384]{3,2,1,0:T(8,128)(2,1)S(1)}, bf16[1,8,40,384]{3,2,1,0:T(8,128)(2,1)}, u32[]{:S(2)}) copy-start(bf16[1,8,40,384]{3,2,1,0:T(8,128)(2,1)} %get-tuple-element.106) | copy-start | bytes 737284
  278.5 17.9 %copy-start.10 = (bf16[1,8,40,384]{3,2,1,0:T(8,128)(2,1)S(1)}, bf16[1,8,40,384]{3,2,1,0:T(8,128)(2,1)}, u32[]{:S(2)}) copy-start(bf16[1,8,40,384]{3,2,1,0:T(8,128)(2,1)} %get-tuple-element.107) | copy-start | bytes 737284
  278.5 18.3 %copy-start.9 = (bf16[1,8,40,384]{3,2,1,0:T(8,128)(2,1)S(1)}, bf16[1,8,40,384]{3,2,1,0:T(8,128)(2,1)}, u32[]{:S(2)}) copy-start(bf16[1,8,40,384]{3,2,1,0:T(8,128)(2,1)} %get-tuple-element.108) | copy-start | bytes 737284
  278.5 18.6 %copy-start.8 = (bf16[1,8,40,384]{3,2,1,0:T(8,128)(2,1)S(1)}, bf16[1,8,40,384]{3,2,1,0:T(8,128)(2,1)}, u32[]{:S(2)}) copy-start(bf16[1,8,40,384]{3,2,1,0:T(8,128)(2,1)} %get-tuple-element.109) | copy-start | bytes 737284
  278.5 18.9 %copy-start.7 = (bf16[1,8,40,384]{3,2,1,0:T(8,128)(2,1)S(1)}, bf16[1,8,40,384]{3,2,1,0:T(8,128)(2,1)}, u32[]{:S(2)}) copy-start(bf16[1,8,40,384]{3,2,1,0:T(8,128)(2,1)} %get-tuple-element.110) | copy-start | bytes 737284
  278.5 19.3 %copy-start.6 = (bf16[1,8,40,384]{3,2,1,0:T(8,128)(2,1)S(1)}, bf16[1,8,40,384]{3,2,1,0:T(8,128)(2,1)}, u32[]{:S(2)}) copy-start(bf16[1,8,40,384]{3,2,1,0:T(8,128)(2,1)} %get-tuple-element.111) | copy-start | bytes 737284
  278.5 19.6 %copy-start.5 = (bf16[1,8,40,384]{3,2,1,0:T(8,128)(2,1)S(1)}, bf16[1,8,40,384]{3,2,1,0:T(8,128)(2,1)}, u32[]{:S(2)}) copy-start(bf16[1,8,40,384]{3,2,1,0:T(8,128)(2,1)} %get-tuple-element.112) | copy-start | bytes 737284
  278.6 20.0 %copy-start.4 = (bf16[1,8,40,384]{3,2,1,0:T(8,128)(2,1)S(1)}, bf16[1,8,40,384]{3,2,1,0:T(8,128)(2,1)}, u32[]{:S(2)}) copy-start(bf16[1,8,40,384]{3,2,1,0:T(8,128)(2,1)} %get-tuple-element.104) | copy-start | bytes 737284
  295.4 10.8 %copy-start.3 = (bf16[1,8,40,384]{3,2,1,0:T(8,128)(2,1)S(1)}, bf16[1,8,40,384]{3,2,1,0:T(8,128)(2,1)}, u32[]{:S(2)}) copy-start(bf16[1,8,40,384]{3,2,1,0:T(8,128)(2,1)} %get-tuple-element.97) | copy-start | bytes 737284
  295.7 10.8 %copy-start.2 = (bf16[1,8,40,384]{3,2,1,0:T(8,128)(2,1)S(1)}, bf16[1,8,40,384]{3,2,1,0:T(8,128)(2,1)}, u32[]{:S(2)}) copy-start(bf16[1,8,40,384]{3,2,1,0:T(8,128)(2,1)} %get-tuple-element.98) | copy-start | bytes 737284
  296.1 10.8 %copy-start.1 = (bf16[1,8,40,384]{3,2,1,0:T(8,128)(2,1)S(1)}, bf16[1,8,40,384]{3,2,1,0:T(8,128)(2,1)}, u32[]{:S(2)}) copy-start(bf16[1,8,40,384]{3,2,1,0:T(8,128)(2,1)} %get-tuple-element.99) | copy-start | bytes 737284
  308.3 3.5 copy-start.14
  308.6 154.9 %copy-start.17 = (f32[384]{0:T(512)S(1)}, f32[384]{0:T(512)}, u32[]{:S(2)}) copy-start(f32[384]{0:T(512)} %param.15) | copy-start | bytes 4612
  308.6 154.9 %copy-start.18 = (f32[384]{0:T(512)S(1)}, f32[384]{0:T(512)}, u32[]{:S(2)}) copy-start(f32[384]{0:T(512)} %param.14) | copy-start | bytes 4612
  463.7 21.9 %collective-permute-start.6 = (bf16[8,1,384]{2,1,0:T(2,128)(2,1)S(1)}, bf16[8,1,384]{2,1,0:T(2,128)(2,1)S(1)}, u32[]{:S(2)}, u32[]{:S(2)}) collective-permute-start(bf16[8,1,384]{2,1,0:T(2,128)(2,1)S(1)} %get-tuple-element.117), channel_id=1, source_target_pairs={{0,1},{1,2},{2,3},{3,4},{4,5},{5,6},{6,7},{7,8},{8,9},{9,10},{10,1... | collective-permute-start | bytes 18440 | tf_op jit(solution)/shard_map/ppermute | solution.py:14
  465.7 20.0 %collective-permute-start.7 = (bf16[8,1,384]{2,1,0:T(2,128)(2,1)S(1)}, bf16[8,1,384]{2,1,0:T(2,128)(2,1)S(1)}, u32[]{:S(2)}, u32[]{:S(2)}) collective-permute-start(bf16[8,1,384]{2,1,0:T(2,128)(2,1)S(1)} %get-tuple-element.118), channel_id=1, source_target_pairs={{1,0},{2,1},{3,2},{4,3},{5,4},{6,5},{7,6},{8,7},{9,8},{10,9},{11,1... | collective-permute-start | bytes 18440 | tf_op jit(solution)/shard_map/ppermute | solution.py:14
  485.8 12.8 %collective-permute-start.8 = (bf16[1,42,384]{2,1,0:T(8,128)(2,1)S(1)}, bf16[1,42,384]{2,1,0:T(8,128)(2,1)S(1)}, u32[]{:S(2)}, u32[]{:S(2)}) collective-permute-start(bf16[1,42,384]{2,1,0:T(8,128)(2,1)S(1)} %get-tuple-element.113), channel_id=1, source_target_pairs={{0,8},{1,9},{2,10},{3,11},{4,12},{5,13},{6,14},{7,15},{8,16},{9,17... | collective-permute-start | bytes 96776 | tf_op jit(solution)/shard_map/ppermute | solution.py:14
  487.7 10.9 %collective-permute-start.9 = (bf16[1,42,384]{2,1,0:T(8,128)(2,1)S(1)}, bf16[1,42,384]{2,1,0:T(8,128)(2,1)S(1)}, u32[]{:S(2)}, u32[]{:S(2)}) collective-permute-start(bf16[1,42,384]{2,1,0:T(8,128)(2,1)S(1)} %get-tuple-element.114), channel_id=1, source_target_pairs={{8,0},{9,1},{10,2},{11,3},{12,4},{13,5},{14,6},{15,7},{16,8},{17,9... | collective-permute-start | bytes 96776 | tf_op jit(solution)/shard_map/ppermute | solution.py:14
  498.7 13.3 %collective-permute-start.10 = (bf16[10,42,384]{2,1,0:T(8,128)(2,1)S(1)}, bf16[10,42,384]{2,1,0:T(8,128)(2,1)S(1)}, u32[]{:S(2)}, u32[]{:S(2)}) collective-permute-start(bf16[10,42,384]{2,1,0:T(8,128)(2,1)S(1)} %pad_maximum_fusion.1), channel_id=1, source_target_pairs={{0,64},{64,128},{128,192},{1,65},{65,129},{129,193},{2,66},{66,130... | collective-permute-start | bytes 967688 | tf_op jit(solution)/shard_map/ppermute | solution.py:14
  514.6 12.4 %collective-permute-start.11 = (bf16[10,42,384]{2,1,0:T(8,128)(2,1)S(1)}, bf16[10,42,384]{2,1,0:T(8,128)(2,1)S(1)}, u32[]{:S(2)}, u32[]{:S(2)}) collective-permute-start(bf16[10,42,384]{2,1,0:T(8,128)(2,1)S(1)} %collective-permute-done.10), channel_id=1, source_target_pairs={{0,64},{64,128},{128,192},{1,65},{65,129},{129,193},{2,66},{66,130... | collective-permute-start | bytes 967688 | tf_op jit(solution)/shard_map/ppermute | solution.py:14
  530.0 3.4 copy-start
  530.0 3.4 copy-start.19
Sparse Core Ops, SparseCore 0:
  46.6 86.8 all-gather.2
  136.2 83.6 all-gather.4
where the time goes:
time: 542 us; the launch traced here: 541 us
  blocking collectives  366 us (68%)
  local copies, waits for them, and re-layouts  66 us (12%)
  waiting for transfers between devices  42.5 us (8%)
  starting transfers between devices  28.6 us (5%)
  matrix products  18.7 us (3%)
  between operations  14.3 us (3%)
    psum x2, blocking collectives, group_act(): total = lax.psum(jnp.sum(grouped, axis=(0, 2)), ('tm', 'space'))  153 us
    psum x2, blocking collectives, group_act(): lax.psum(jnp.sum(centered * centered, axis=(0, 2)), ('tm', 'space'))  148 us
    slice x4, local copies, waits for them, and re-layouts, apply_taps(): kernel[step_t, step_y, step_x]  47.1 us
    ppermute x12, waiting for transfers between devices, shifted(): lax.ppermute(value, axis, [(source, source + steps) for source in range(i...  42.5 us
    all_gather x1, blocking collectives, shards(): lax.all_gather(kernel_first, 'tm', axis=4, tiled=True)  32.9 us
    all_gather x1, blocking collectives, shards(): lax.all_gather(kernel_second, 'tm', axis=4, tiled=True)  32 us
    ppermute x12, starting transfers between devices, shifted(): lax.ppermute(value, axis, [(source, source + steps) for source in range(i...  28.6 us
    dot_general x54, matrix products, apply_taps(): jnp.dot(window.reshape(-1, width), kernel[step_t, step_y, step_x], prefer...  18.7 us
  transfers between devices with their start and end apart: 14, of which 6 were waited for; matrix products, arithmetic and copies ran while one was open for 14% of the time, Pallas kernels for 0%

commit v1 on v0

--- a/solution.py
+++ b/solution.py
@@ -6,6 +6,9 @@
 GROUPS = 32
 GX = 8
 EPS = 1e-06
+do_ticks = lambda frame_in: jnp.concatenate(
+    lax.all_to_all(jnp.stack(lax.psum(1, "tm") * [frame_in]), "tm", 0, 0), axis=4
+)
 
 
 def shifted(value, axis, steps):
@@ -88,7 +91,7 @@
     first_act = group_act(tile, gain_first, shift_first, count)
     cols_first, cols_second = (
         lax.all_gather(kernel_first, "tm", axis=4, tiled=True),
-        lax.all_gather(kernel_second, "tm", axis=4, tiled=True),
+        do_ticks(kernel_second),
     )
     first_out = conv_near(first_act, cols_first, bias_first)
     second_act = group_act(first_out, gain_second, shift_second, count)

time: 542 us -> 512 us (0.945)
  blocking collectives: 366 us -> 344 us
  waiting for transfers between devices: 42.5 us -> 35.3 us
    all_gather x1 -> x0, blocking collectives: 32 us -> none  [shards(): lax.all_gather(kernel_second, 'tm', axis=4, tiled=True)]
    all_to_all x0 -> x1, blocking collectives: none -> 8.7 us  [lax.all_to_all(jnp.stack(lax.psum(1, 'tm') * [frame_in]), 'tm', 0, 0)]
    ppermute x12, waiting for transfers between devices: 42.5 us -> 35.2 us  [shifted(): lax.ppermute(value, axis, [(source, source + steps) for source in range(i...]
  transfers between devices with their start and end apart: 14 -> 14, of which waited for: 6 -> 7; matrix products, arithmetic and copies ran while one was open for 14% -> 13% of each run, Pallas kernels for 0% -> 0%
where the time goes in v1:
time: 512 us; the launch traced here: 506 us
  blocking collectives  344 us (67%)
  local copies, waits for them, and re-layouts  60.9 us (12%)
  waiting for transfers between devices  35.3 us (7%)
  starting transfers between devices  28.5 us (6%)
  matrix products  18.7 us (4%)
  between operations  14.3 us (3%)
  other arithmetic  5.27 us (1%)
    psum x2, blocking collectives, group_act(): total = lax.psum(jnp.sum(grouped, axis=(0, 2)), ('tm', 'space'))  154 us
    psum x2, blocking collectives, group_act(): lax.psum(jnp.sum(centered * centered, axis=(0, 2)), ('tm', 'space'))  148 us
    slice x4, local copies, waits for them, and re-layouts, apply_taps(): kernel[step_t, step_y, step_x]  47.2 us
    ppermute x12, waiting for transfers between devices, shifted(): lax.ppermute(value, axis, [(source, source + steps) for source in range(i...  35.2 us
    all_gather x1, blocking collectives, shards(): lax.all_gather(kernel_first, 'tm', axis=4, tiled=True)  32.9 us
    ppermute x12, starting transfers between devices, shifted(): lax.ppermute(value, axis, [(source, source + steps) for source in range(i...  28.5 us
    dot_general x54, matrix products, apply_taps(): jnp.dot(window.reshape(-1, width), kernel[step_t, step_y, step_x], prefer...  18.7 us
  transfers between devices with their start and end apart: 14, of which 7 were waited for; matrix products, arithmetic and copies ran while one was open for 13% of the time, Pallas kernels for 0%

profile of v1, /device:TPU:62, one launch (start us, length us, event | category | flops | bytes accessed | tf_op | source)
XLA Modules:
  0.0 506.5 jit_solution(5880331351095292506)
XLA Ops:
  6.5 2.2 copy.14
  8.8 32.9 %all_gather.9 = bf16[3,3,3,6,384]{3,2,1,0,4:T(4,128)(2,1)S(1)} all-gather(bf16[3,3,3,6,96]{3,2,1,0,4:T(4,128)(2,1)} %copy.14), channel_id=1, replica_groups=mesh['tm'=4,'space'=64] {'tm'}, dimensions={4}, use_global_device_ids=true | all-gather | bytes 155520 | tf_op jit(solution)/shard_map/all_gather | solution.py:93
  41.7 4.8 copy.15
  46.5 0.8 stack.29
  47.4 8.7 %all_to_all.5 = bf16[4,3,3,3,6,96]{5,4,3,2,1,0:T(8,128)(2,1)S(1)} all-to-all(bf16[4,3,3,3,6,96]{5,4,3,2,1,0:T(8,128)(2,1)S(1)} %stack.29), channel_id=1, replica_groups=mesh['tm'=4,'space'=64] {'tm'}, dimensions={0} | all-to-all | bytes 248832 | tf_op jit(solution)/shard_map/all_to_all | solution.py:10
  56.2 0.9 reshape.283
  57.1 1.0 convert_reduce_fusion
  58.4 76.2 %psum.28 = f32[32]{0:T(128)S(1)} all-reduce(f32[32]{0:T(128)S(1)} %reduce_sum.51), channel_id=1, replica_groups=mesh['tm'=4,'space'=64] {'tm','space'}, use_global_device_ids=true, to_apply=%region_2.0 | all-reduce | flops 32 | bytes 256 | tf_op jit(solution)/shard_map/psum | solution.py:35
  134.7 1.0 fusion.35
  136.0 74.7 %psum.29 = f32[32]{0:T(128)S(1)} all-reduce(f32[32]{0:T(128)S(1)} %reduce_sum.54), channel_id=1, replica_groups=mesh['tm'=4,'space'=64] {'tm','space'}, use_global_device_ids=true, to_apply=%region_5.6 | all-reduce | flops 32 | bytes 256 | tf_op jit(solution)/shard_map/psum | solution.py:38
  210.9 1.1 fusion.46
  212.1 1.9 collective-permute-start
  214.0 3.6 collective-permute-start.1
  217.7 1.3 collective-permute-done.1
  219.1 3.5 collective-permute-start.2
  222.6 2.4 collective-permute-start.3
  225.0 3.5 collective-permute-done.3
  228.6 1.3 collective-permute-start.4
  230.0 8.4 %collective-permute-done.4 = bf16[10,42,384]{2,1,0:T(8,128)(2,1)S(1)} collective-permute-done((bf16[10,42,384]{2,1,0:T(8,128)(2,1)S(1)}, bf16[10,42,384]{2,1,0:T(8,128)(2,1)S(1)}, u32[]{:S(2)}, u32[]{:S(2)}) %collective-permute-start.4) | collective-permute-done | bytes 322592 | tf_op jit(solution)/shard_map/ppermute | solution.py:17
  238.4 1.3 collective-permute-start.5
  239.9 1.4 fusion.92
  241.4 7.8 %collective-permute-done.5 = bf16[10,42,384]{2,1,0:T(8,128)(2,1)S(1)} collective-permute-done((bf16[10,42,384]{2,1,0:T(8,128)(2,1)S(1)}, bf16[10,42,384]{2,1,0:T(8,128)(2,1)S(1)}, u32[]{:S(2)}, u32[]{:S(2)}) %collective-permute-start.5) | collective-permute-done | bytes 322592 | tf_op jit(solution)/shard_map/ppermute | solution.py:17
  249.2 1.1 fusion.91
  250.4 16.8 %fusion.85 = (bf16[1,1,1,384,384]{4,2,1,0,3:T(2,128)(2,1)S(1)}, bf16[1,1,1,384,384]{4,2,1,0,3:T(2,128)(2,1)S(1)}, bf16[1,1,1,384,384]{4,2,1,0,3:T(2,128)(2,1)S(1...) fusion(bf16[3,3,3,384,384]{4,2,1,0,3:T(4,128)(2,1)} %all-gather, ...), kind=kLoop, calls=%fused_computation.180 | loop fusion | bytes 11206656 | tf_op jit(solution)/shard_map/slice | solution.py:55
  271.0 7.0 %fusion.86 = (bf16[1,1,1,384,384]{4,2,1,0,3:T(2,128)(2,1)S(1)}, bf16[1,1,1,384,384]{4,2,1,0,3:T(2,128)(2,1)S(1)}, bf16[1,1,1,384,384]{4,2,1,0,3:T(2,128)(2,1)S(1...) fusion(bf16[3,3,3,384,384]{4,2,1,0,3:T(4,128)(2,1)} %all-gather, ...), kind=kLoop, calls=%fused_computation.181 | loop fusion | bytes 4718592 | tf_op jit(solution)/shard_map/slice | solution.py:55
  279.4 0.3 fusion.80
  280.5 0.8 fusion.27
  281.3 0.3 convolution_add_fusion.16
  283.6 0.4 add_reduce_fusion
  284.2 77.9 %psum.30 = f32[32]{0:T(128)S(1)} all-reduce(f32[32]{0:T(128)S(1)} %reduce_sum.72), channel_id=1, replica_groups=mesh['tm'=4,'space'=64] {'tm','space'}, use_global_device_ids=true, to_apply=%region_8.9 | all-reduce | flops 32 | bytes 256 | tf_op jit(solution)/shard_map/psum | solution.py:35
  362.6 73.1 %psum.31 = f32[32]{0:T(128)S(1)} all-reduce(f32[32]{0:T(128)S(1)} %reduce_sum.75), channel_id=1, replica_groups=mesh['tm'=4,'space'=64] {'tm','space'}, use_global_device_ids=true, to_apply=%region_11.12 | all-reduce | flops 32 | bytes 256 | tf_op jit(solution)/shard_map/psum | solution.py:38
  436.1 1.9 collective-permute-start.6
  438.1 3.6 collective-permute-start.7
  441.8 1.4 collective-permute-done.7
  443.2 4.2 collective-permute-start.8
  447.4 1.9 collective-permute-start.9
  449.4 3.9 collective-permute-done.9
  453.4 1.3 collective-permute-start.10
  455.1 16.4 %fusion.83 = (bf16[1,1,1,384,384]{4,2,1,0,3:T(2,128)(2,1)S(1)}, bf16[1,1,1,384,384]{4,2,1,0,3:T(2,128)(2,1)S(1)}, bf16[1,1,1,384,384]{4,2,1,0,3:T(2,128)(2,1)S(1...) fusion(bf16[3,3,3,384,384]{4,2,1,0,3:T(4,128)(2,1)} %all-gather, ...), kind=kLoop, calls=%fused_computation.178 | loop fusion | bytes 11206656 | tf_op jit(solution)/shard_map/slice | solution.py:55
  471.5 7.0 %fusion.84 = (bf16[1,1,1,384,384]{4,2,1,0,3:T(2,128)(2,1)S(1)}, bf16[1,1,1,384,384]{4,2,1,0,3:T(2,128)(2,1)S(1)}, bf16[1,1,1,384,384]{4,2,1,0,3:T(2,128)(2,1)S(1...) fusion(bf16[3,3,3,384,384]{4,2,1,0,3:T(4,128)(2,1)} %all-gather, ...), kind=kLoop, calls=%fused_computation.179 | loop fusion | bytes 4718592 | tf_op jit(solution)/shard_map/slice | solution.py:55
  479.4 0.3 fusion.55
  480.1 0.3 fusion.53
  480.7 0.3 fusion.51
  481.4 1.6 collective-permute-start.11
  483.3 0.3 fusion.48
  483.6 8.9 %collective-permute-done.11 = bf16[10,42,384]{2,1,0:T(8,128)(2,1)S(1)} collective-permute-done((bf16[10,42,384]{2,1,0:T(8,128)(2,1)S(1)}, bf16[10,42,384]{2,1,0:T(8,128)(2,1)S(1)}, u32[]{:S(2)}, u32[]{:S(2)}) %collective-permute-start.11) | collective-permute-done | bytes 322592 | tf_op jit(solution)/shard_map/ppermute | solution.py:17
  495.5 0.7 fusion.33
  498.9 0.8 fusion.36
  (135 shorter events, 18.8 us)
Async XLA Ops:
  6.5 204.4 %copy-start.16 = (f32[384]{0:T(512)S(1)}, f32[384]{0:T(512)}, u32[]{:S(2)}) copy-start(f32[384]{0:T(512)} %param.10) | copy-start | bytes 4612
  6.5 204.4 %copy-start.15 = (f32[384]{0:T(512)S(1)}, f32[384]{0:T(512)}, u32[]{:S(2)}) copy-start(f32[384]{0:T(512)} %param.11) | copy-start | bytes 4612
  6.5 243.8 %all-gather.3.cloned.1.call-start = ((), (), s32[]{:S(2)}) async-start(), calls=%async_computation.1 | async-start | bytes 10782720 | tf_op jit(solution)/shard_map/all_gather | solution.py:72
  46.5 408.6 %all-gather.5.cloned.1.call-start = ((), (), s32[]{:S(2)}) async-start(), calls=%async_computation.2 | async-start | bytes 10782720 | tf_op jit(solution)/shard_map/all_gather | solution.py:72
  212.1 5.6 %collective-permute-start = (bf16[8,1,384]{2,1,0:T(2,128)(2,1)S(1)}, bf16[8,1,384]{2,1,0:T(2,128)(2,1)S(1)}, u32[]{:S(2)}, u32[]{:S(2)}) collective-permute-start(bf16[8,1,384]{2,1,0:T(2,128)(2,1)S(1)} %get-tuple-element.119), channel_id=1, source_target_pairs={{0,1},{1,2},{2,3},{3,4},{4,5},{5,6},{6,7},{7,8},{8,9},{9,10},{10,1... | collective-permute-start | bytes 18440 | tf_op jit(solution)/shard_map/ppermute | solution.py:17
  214.0 5.0 collective-permute-start.1
  219.1 5.9 %collective-permute-start.2 = (bf16[1,42,384]{2,1,0:T(8,128)(2,1)S(1)}, bf16[1,42,384]{2,1,0:T(8,128)(2,1)S(1)}, u32[]{:S(2)}, u32[]{:S(2)}) collective-permute-start(bf16[1,42,384]{2,1,0:T(8,128)(2,1)S(1)} %get-tuple-element.115), channel_id=1, source_target_pairs={{0,8},{1,9},{2,10},{3,11},{4,12},{5,13},{6,14},{7,15},{8,16},{9,17... | collective-permute-start | bytes 96776 | tf_op jit(solution)/shard_map/ppermute | solution.py:17
  222.6 5.9 %collective-permute-start.3 = (bf16[1,42,384]{2,1,0:T(8,128)(2,1)S(1)}, bf16[1,42,384]{2,1,0:T(8,128)(2,1)S(1)}, u32[]{:S(2)}, u32[]{:S(2)}) collective-permute-start(bf16[1,42,384]{2,1,0:T(8,128)(2,1)S(1)} %get-tuple-element.116), channel_id=1, source_target_pairs={{8,0},{9,1},{10,2},{11,3},{12,4},{13,5},{14,6},{15,7},{16,8},{17,9... | collective-permute-start | bytes 96776 | tf_op jit(solution)/shard_map/ppermute | solution.py:17
  228.6 9.8 %collective-permute-start.4 = (bf16[10,42,384]{2,1,0:T(8,128)(2,1)S(1)}, bf16[10,42,384]{2,1,0:T(8,128)(2,1)S(1)}, u32[]{:S(2)}, u32[]{:S(2)}) collective-permute-start(bf16[10,42,384]{2,1,0:T(8,128)(2,1)S(1)} %pad_maximum_fusion), channel_id=1, source_target_pairs={{0,64},{64,128},{128,192},{1,65},{65,129},{129,193},{2,66},{66,130... | collective-permute-start | bytes 967688 | tf_op jit(solution)/shard_map/ppermute | solution.py:17
  238.4 10.8 %collective-permute-start.5 = (bf16[10,42,384]{2,1,0:T(8,128)(2,1)S(1)}, bf16[10,42,384]{2,1,0:T(8,128)(2,1)S(1)}, u32[]{:S(2)}, u32[]{:S(2)}) collective-permute-start(bf16[10,42,384]{2,1,0:T(8,128)(2,1)S(1)} %collective-permute-done.4), channel_id=1, source_target_pairs={{0,64},{64,128},{128,192},{1,65},{65,129},{129,193},{2,66},{66,130... | collective-permute-start | bytes 967688 | tf_op jit(solution)/shard_map/ppermute | solution.py:17
  250.3 16.9 %copy-start.13 = (bf16[1,8,40,384]{3,2,1,0:T(8,128)(2,1)S(1)}, bf16[1,8,40,384]{3,2,1,0:T(8,128)(2,1)}, u32[]{:S(2)}) copy-start(bf16[1,8,40,384]{3,2,1,0:T(8,128)(2,1)} %get-tuple-element.96) | copy-start | bytes 737284
  250.3 17.3 %copy-start.12 = (bf16[1,8,40,384]{3,2,1,0:T(8,128)(2,1)S(1)}, bf16[1,8,40,384]{3,2,1,0:T(8,128)(2,1)}, u32[]{:S(2)}) copy-start(bf16[1,8,40,384]{3,2,1,0:T(8,128)(2,1)} %get-tuple-element.105) | copy-start | bytes 737284
  250.3 17.6 %copy-start.11 = (bf16[1,8,40,384]{3,2,1,0:T(8,128)(2,1)S(1)}, bf16[1,8,40,384]{3,2,1,0:T(8,128)(2,1)}, u32[]{:S(2)}) copy-start(bf16[1,8,40,384]{3,2,1,0:T(8,128)(2,1)} %get-tuple-element.106) | copy-start | bytes 737284
  250.3 17.9 %copy-start.10 = (bf16[1,8,40,384]{3,2,1,0:T(8,128)(2,1)S(1)}, bf16[1,8,40,384]{3,2,1,0:T(8,128)(2,1)}, u32[]{:S(2)}) copy-start(bf16[1,8,40,384]{3,2,1,0:T(8,128)(2,1)} %get-tuple-element.107) | copy-start | bytes 737284
  250.3 18.3 %copy-start.9 = (bf16[1,8,40,384]{3,2,1,0:T(8,128)(2,1)S(1)}, bf16[1,8,40,384]{3,2,1,0:T(8,128)(2,1)}, u32[]{:S(2)}) copy-start(bf16[1,8,40,384]{3,2,1,0:T(8,128)(2,1)} %get-tuple-element.108) | copy-start | bytes 737284
  250.4 18.6 %copy-start.8 = (bf16[1,8,40,384]{3,2,1,0:T(8,128)(2,1)S(1)}, bf16[1,8,40,384]{3,2,1,0:T(8,128)(2,1)}, u32[]{:S(2)}) copy-start(bf16[1,8,40,384]{3,2,1,0:T(8,128)(2,1)} %get-tuple-element.109) | copy-start | bytes 737284
  250.4 19.0 %copy-start.7 = (bf16[1,8,40,384]{3,2,1,0:T(8,128)(2,1)S(1)}, bf16[1,8,40,384]{3,2,1,0:T(8,128)(2,1)}, u32[]{:S(2)}) copy-start(bf16[1,8,40,384]{3,2,1,0:T(8,128)(2,1)} %get-tuple-element.110) | copy-start | bytes 737284
  250.4 19.3 %copy-start.6 = (bf16[1,8,40,384]{3,2,1,0:T(8,128)(2,1)S(1)}, bf16[1,8,40,384]{3,2,1,0:T(8,128)(2,1)}, u32[]{:S(2)}) copy-start(bf16[1,8,40,384]{3,2,1,0:T(8,128)(2,1)} %get-tuple-element.111) | copy-start | bytes 737284
  250.4 19.6 %copy-start.5 = (bf16[1,8,40,384]{3,2,1,0:T(8,128)(2,1)S(1)}, bf16[1,8,40,384]{3,2,1,0:T(8,128)(2,1)}, u32[]{:S(2)}) copy-start(bf16[1,8,40,384]{3,2,1,0:T(8,128)(2,1)} %get-tuple-element.112) | copy-start | bytes 737284
  250.4 20.0 %copy-start.4 = (bf16[1,8,40,384]{3,2,1,0:T(8,128)(2,1)S(1)}, bf16[1,8,40,384]{3,2,1,0:T(8,128)(2,1)}, u32[]{:S(2)}) copy-start(bf16[1,8,40,384]{3,2,1,0:T(8,128)(2,1)} %get-tuple-element.104) | copy-start | bytes 737284
  267.2 10.9 %copy-start.3 = (bf16[1,8,40,384]{3,2,1,0:T(8,128)(2,1)S(1)}, bf16[1,8,40,384]{3,2,1,0:T(8,128)(2,1)}, u32[]{:S(2)}) copy-start(bf16[1,8,40,384]{3,2,1,0:T(8,128)(2,1)} %get-tuple-element.97) | copy-start | bytes 737284
  267.6 10.8 %copy-start.2 = (bf16[1,8,40,384]{3,2,1,0:T(8,128)(2,1)S(1)}, bf16[1,8,40,384]{3,2,1,0:T(8,128)(2,1)}, u32[]{:S(2)}) copy-start(bf16[1,8,40,384]{3,2,1,0:T(8,128)(2,1)} %get-tuple-element.98) | copy-start | bytes 737284
  267.9 10.8 %copy-start.1 = (bf16[1,8,40,384]{3,2,1,0:T(8,128)(2,1)S(1)}, bf16[1,8,40,384]{3,2,1,0:T(8,128)(2,1)}, u32[]{:S(2)}) copy-start(bf16[1,8,40,384]{3,2,1,0:T(8,128)(2,1)} %get-tuple-element.99) | copy-start | bytes 737284
  280.1 3.5 copy-start.14
  280.5 155.4 %copy-start.17 = (f32[384]{0:T(512)S(1)}, f32[384]{0:T(512)}, u32[]{:S(2)}) copy-start(f32[384]{0:T(512)} %param.15) | copy-start | bytes 4612
  280.5 155.4 %copy-start.18 = (f32[384]{0:T(512)S(1)}, f32[384]{0:T(512)}, u32[]{:S(2)}) copy-start(f32[384]{0:T(512)} %param.14) | copy-start | bytes 4612
  436.1 5.6 %collective-permute-start.6 = (bf16[8,1,384]{2,1,0:T(2,128)(2,1)S(1)}, bf16[8,1,384]{2,1,0:T(2,128)(2,1)S(1)}, u32[]{:S(2)}, u32[]{:S(2)}) collective-permute-start(bf16[8,1,384]{2,1,0:T(2,128)(2,1)S(1)} %get-tuple-element.117), channel_id=1, source_target_pairs={{0,1},{1,2},{2,3},{3,4},{4,5},{5,6},{6,7},{7,8},{8,9},{9,10},{10,1... | collective-permute-start | bytes 18440 | tf_op jit(solution)/shard_map/ppermute | solution.py:17
  438.1 5.1 %collective-permute-start.7 = (bf16[8,1,384]{2,1,0:T(2,128)(2,1)S(1)}, bf16[8,1,384]{2,1,0:T(2,128)(2,1)S(1)}, u32[]{:S(2)}, u32[]{:S(2)}) collective-permute-start(bf16[8,1,384]{2,1,0:T(2,128)(2,1)S(1)} %get-tuple-element.118), channel_id=1, source_target_pairs={{1,0},{2,1},{3,2},{4,3},{5,4},{6,5},{7,6},{8,7},{9,8},{10,9},{11,1... | collective-permute-start | bytes 18440 | tf_op jit(solution)/shard_map/ppermute | solution.py:17
  443.2 6.1 %collective-permute-start.8 = (bf16[1,42,384]{2,1,0:T(8,128)(2,1)S(1)}, bf16[1,42,384]{2,1,0:T(8,128)(2,1)S(1)}, u32[]{:S(2)}, u32[]{:S(2)}) collective-permute-start(bf16[1,42,384]{2,1,0:T(8,128)(2,1)S(1)} %get-tuple-element.113), channel_id=1, source_target_pairs={{0,8},{1,9},{2,10},{3,11},{4,12},{5,13},{6,14},{7,15},{8,16},{9,17... | collective-permute-start | bytes 96776 | tf_op jit(solution)/shard_map/ppermute | solution.py:17
  447.4 5.9 %collective-permute-start.9 = (bf16[1,42,384]{2,1,0:T(8,128)(2,1)S(1)}, bf16[1,42,384]{2,1,0:T(8,128)(2,1)S(1)}, u32[]{:S(2)}, u32[]{:S(2)}) collective-permute-start(bf16[1,42,384]{2,1,0:T(8,128)(2,1)S(1)} %get-tuple-element.114), channel_id=1, source_target_pairs={{8,0},{9,1},{10,2},{11,3},{12,4},{13,5},{14,6},{15,7},{16,8},{17,9... | collective-permute-start | bytes 96776 | tf_op jit(solution)/shard_map/ppermute | solution.py:17
  453.4 25.4 %collective-permute-start.10 = (bf16[10,42,384]{2,1,0:T(8,128)(2,1)S(1)}, bf16[10,42,384]{2,1,0:T(8,128)(2,1)S(1)}, u32[]{:S(2)}, u32[]{:S(2)}) collective-permute-start(bf16[10,42,384]{2,1,0:T(8,128)(2,1)S(1)} %pad_maximum_fusion.1), channel_id=1, source_target_pairs={{0,64},{64,128},{128,192},{1,65},{65,129},{129,193},{2,66},{66,130... | collective-permute-start | bytes 967688 | tf_op jit(solution)/shard_map/ppermute | solution.py:17
  481.4 11.1 %collective-permute-start.11 = (bf16[10,42,384]{2,1,0:T(8,128)(2,1)S(1)}, bf16[10,42,384]{2,1,0:T(8,128)(2,1)S(1)}, u32[]{:S(2)}, u32[]{:S(2)}) collective-permute-start(bf16[10,42,384]{2,1,0:T(8,128)(2,1)S(1)} %collective-permute-done.10), channel_id=1, source_target_pairs={{0,64},{64,128},{128,192},{1,65},{65,129},{129,193},{2,66},{66,130... | collective-permute-start | bytes 967688 | tf_op jit(solution)/shard_map/ppermute | solution.py:17
  495.5 3.4 copy-start
  495.5 3.4 copy-start.19
Sparse Core Ops, SparseCore 0:
  46.6 86.4 all-gather.2
  135.8 83.7 all-gather.4
